TPU v7x, 32 devices: a whole 2x2x4 slice. The times are simulated.
32 devices in a mesh: feat: 4 (over x, core), samp: 8 (over z, y).
Axes of the slice: x: 2, y: 2, z: 4, core: 2. Of those that a mesh axis runs over, the one named last changes fastest.
Arguments:
- tier_one: bfloat16 [8192, 3072], P('feat', 'samp')
- residuals: bfloat16 [3072, 128], P('samp'), may hold values from -6 to 6
- pair_list: int32 [3, 16384], P(None, 'feat'), may hold values from 0 to 8191, as said below
Outputs:
- scores: float32 [16384, 128], P(('feat', 'samp'))
Inputs may be any that keep to these rules, and one draw needn't show every extreme that they name: `pair_list`: rows 0 and 1 are feature indices, row 2 an operator id of 0 to 3; each descriptor's two features differ.
All inputs are finite; a program needn't handle non-finite values.
Results may differ from a plain program's by a relative error of at most 0.0031.
Values may be sent and summed in bfloat16 or wider, within the bound.
A program may use at most 64 MiB of HBM per device.

v0:
```python
import functools
import math

import jax
import jax.numpy as jnp
from jax import lax
from jax.experimental import pallas as pl
from jax.experimental.pallas import tpu as pltpu
from jax.sharding import PartitionSpec as P

epsilon = 1e-05
MESH = pl.DeviceIdType.MESH
lanes = 128


def kernel(
    sizes, tier_ref, res_ref, pair_smem, pair_vmem, out_ref,
    slots, table, first_even, second_even, first_odd, second_odd,
    op_wide, weights, share_block, stats_wide,
    near_out, near_in, line_out, line_in, send_stats, recv_stats, turned, scale,
    own_sem, cross_send, cross_recv, sib_send, sib_recv, relay_send, relay_recv,
    near_send, near_recv, line_send, line_recv, stats_send, stats_recv,
):
    n_feat, n_samp, rows, samples, pairs, chunks = sizes
    chips = n_feat // 2
    pieces = samples // lanes
    owned = pairs // n_samp
    sub = min(owned // 2, 128)
    group, tall = 8, 16
    step = rows // chunks
    total_samples = samples * n_samp
    feat = lax.axis_index("feat")
    samp = lax.axis_index("samp")
    chip = feat // 2
    core = lax.rem(feat, 2)
    sibling = chip * 2 + 1 - core
    half = n_samp // 2
    high = samp // 2
    low = lax.rem(samp, 2)
    partner = high * 2 + 1 - low

    def far(offset):
        return lax.rem(chip + offset, chips) * 2 + core

    barrier = pltpu.get_barrier_semaphore()
    pl.semaphore_signal(barrier, inc=1, device_id=(sibling, samp), device_id_type=MESH)
    for offset in range(1, chips):
        pl.semaphore_signal(barrier, inc=1, device_id=(far(offset), samp), device_id_type=MESH)
    for offset in range(1, n_samp):
        pl.semaphore_signal(
            barrier, inc=1, device_id=(feat, lax.rem(samp + offset, n_samp)), device_id_type=MESH
        )
    own_copy = pltpu.make_async_copy(tier_ref, slots.at[feat], own_sem)
    own_copy.start()
    pl.semaphore_wait(barrier, 1 + (chips - 1) + (n_samp - 1))

    def part(index):
        return pl.ds(pl.multiple_of(index * step, step), step)

    def cross(offset, k, holder, target):
        return pltpu.make_async_remote_copy(
            src_ref=tier_ref.at[part(k)],
            dst_ref=slots.at[holder, part(k)],
            send_sem=cross_send.at[offset - 1, k],
            recv_sem=cross_recv.at[offset - 1, k],
            device_id=(target, samp),
            device_id_type=MESH,
        )

    def relay(offset, k, holder):
        return pltpu.make_async_remote_copy(
            src_ref=slots.at[holder, part(k)],
            dst_ref=slots.at[holder, part(k)],
            send_sem=relay_send.at[offset - 1, k],
            recv_sem=relay_recv.at[offset - 1, k],
            device_id=(sibling, samp),
            device_id_type=MESH,
        )

    def to_sibling(holder):
        return pltpu.make_async_remote_copy(
            src_ref=tier_ref,
            dst_ref=slots.at[holder],
            send_sem=sib_send,
            recv_sem=sib_recv,
            device_id=(sibling, samp),
            device_id_type=MESH,
        )

    for offset in range(1, chips):
        @pl.loop(0, chunks)
        def _(k):
            cross(offset, k, feat, far(offset)).start()
    to_sibling(feat).start()

    flat = table.reshape(n_feat * rows * 4, lanes)

    def widen(holder, k):
        @pl.loop(0, step // 64 if step % 64 == 0 else 1)
        def _(g):
            size = 64 if step % 64 == 0 else step
            start = pl.multiple_of(k * step + g * size, size)
            for j in range(pieces):
                values = slots[holder, pl.ds(start, size), j * lanes:(j + 1) * lanes]
                flat[pl.ds(4 * (holder * rows + start) + j, size, stride=4), :] = values.astype(jnp.float32)

    weights[:, :lanes] = res_ref[...]
    weights[:, lanes:] = jnp.ones((samples, lanes), jnp.bfloat16)
    col_local = jnp.sum(res_ref[...].astype(jnp.float32), axis=0, keepdims=True)

    @pl.loop(0, pairs // lanes)
    def _(g):
        span = pl.ds(pl.multiple_of(g * lanes, lanes), lanes)
        op_wide[span, :] = jnp.broadcast_to(pair_vmem[2:3, span], (lanes, lanes)).T

    own_copy.wait()

    @pl.loop(0, chunks)
    def _(k):
        widen(feat, k)

    to_sibling(sibling).wait_recv()

    @pl.loop(0, chunks)
    def _(k):
        widen(sibling, k)

    for offset in range(1, chips):
        mine = far(chips - offset)
        theirs = mine + 1 - 2 * core

        @pl.loop(0, chunks)
        def _(k):
            cross(offset, k, mine, feat).wait_recv()
            relay(offset, k, mine).start()
            widen(mine, k)

            @pl.when(k > 0)
            def _():
                relay(offset, k - 1, theirs).wait_recv()
                widen(theirs, k - 1)

        relay(offset, chunks - 1, theirs).wait_recv()
        widen(theirs, chunks - 1)

    lane_id = lax.broadcasted_iota(jnp.int32, (sub, lanes), 1)

    def owner_of(b):
        return lax.rem(high + 1 + b, half) * 2 + lax.rem(low + 1 + b // half, 2)

    def gather(stages, base, p):
        firsts = [table[pair_smem[0, base + p + u]] for u in range(group)]
        seconds = [table[pair_smem[1, base + p + u]] for u in range(group)]
        for u in range(group):
            stages[0][4 * (p + u):4 * (p + u) + 4, :] = firsts[u]
            stages[1][4 * (p + u):4 * (p + u) + 4, :] = seconds[u]

    def build(stages, base, p):
        op = op_wide[pl.ds(pl.multiple_of(base + p, tall), tall), :]
        parts = []
        square = jnp.zeros((tall, lanes), jnp.float32)
        for j in range(pieces):
            a = stages[0][pl.ds(4 * p + j, tall, stride=4), :]
            b = stages[1][pl.ds(4 * p + j, tall, stride=4), :]
            plain = a + jnp.where(op == 1, -b, b)
            other = jnp.where(op == 2, a * b, a / (1.0 + jnp.abs(b)))
            built = jnp.where(op < 2, plain, other).astype(jnp.bfloat16)
            parts.append(built)
            wide = built.astype(jnp.float32)
            square += wide * wide
        return jnp.concatenate(parts, axis=1), jnp.sum(square, axis=1, keepdims=True)

    def advance(now, base, later, next_base, here):
        built, squares = [], []
        steps = sub // tall
        share = sub // 2 // steps
        for i in range(steps):
            one, square = build(now, base, i * tall)
            built.append(one)
            squares.append(square)
            for p in range(i * share, (i + 1) * share, group):
                gather(later, next_base, p)
        both = jnp.dot(
            jnp.concatenate(built, axis=0), weights[...], preferred_element_type=jnp.float32
        )
        for p in range(sub // 2, sub, group):
            gather(later, next_base, p)
        sums = both[:, lanes:]
        share_block[here, :] = both[:, :lanes] - sums * (col_local / samples)
        stats_wide[here, :] = jnp.where(lane_id == 0, sums, jnp.concatenate(squares, axis=0))

    even = (first_even, second_even)
    odd = (first_odd, second_odd)

    @pl.loop(0, sub // group)
    def _(g):
        base = owner_of(0) * owned
        firsts = [table[pair_smem[0, base + g * group + u]] for u in range(group)]
        seconds = [table[pair_smem[1, base + g * group + u]] for u in range(group)]
        for u in range(group):
            spot = pl.ds(pl.multiple_of((g * group + u) * 4, 4), 4)
            first_even[spot, :] = firsts[u]
            second_even[spot, :] = seconds[u]

    couples = owned // (2 * sub)

    def make_block(b, owner):
        @pl.loop(0, couples)
        def _(h):
            base = owner * owned + h * (2 * sub)
            after = b * couples + h + 1
            next_base = owner_of(after // couples) * owned + lax.rem(after, couples) * (2 * sub)
            first_half = pl.ds(pl.multiple_of(h * (2 * sub), sub), sub)
            second_half = pl.ds(pl.multiple_of(h * (2 * sub) + sub, sub), sub)
            advance(even, base, odd, base + sub, first_half)
            advance(odd, base + sub, even, next_base, second_half)

        for q in range(owned // lanes):
            flipped = stats_wide[q * lanes:(q + 1) * lanes, :].T
            send_stats[owner, 0:2, q * lanes:(q + 1) * lanes] = flipped[0:2, :]
        send_stats[owner, 2:3, 0:lanes] = col_local

    def near_copy(t):
        return pltpu.make_async_remote_copy(
            src_ref=near_out.at[t],
            dst_ref=near_in.at[t],
            send_sem=near_send.at[t],
            recv_sem=near_recv.at[t],
            device_id=(feat, partner),
            device_id_type=MESH,
        )

    def line_copy(t, source, target):
        return pltpu.make_async_remote_copy(
            src_ref=line_out.at[t],
            dst_ref=line_in.at[source],
            send_sem=line_send.at[t],
            recv_sem=line_recv.at[source],
            device_id=(feat, target * 2 + low),
            device_id_type=MESH,
        )

    def stats_copy(owner, source):
        return pltpu.make_async_remote_copy(
            src_ref=send_stats.at[owner],
            dst_ref=recv_stats.at[source],
            send_sem=stats_send.at[owner],
            recv_sem=stats_recv.at[source],
            device_id=(feat, owner),
            device_id_type=MESH,
        )

    @pl.loop(0, n_samp)
    def _(b):
        owner = owner_of(b)
        make_block(b, owner)

        @pl.when(b < half)
        def _():
            near_out[b] = share_block[...].astype(jnp.bfloat16)
            near_copy(b).start()
            stats_copy(owner, samp).start()

        @pl.when(b >= half)
        def _():
            t = b - half
            near_copy(t).wait_recv()
            total = share_block[...] + near_in[t].astype(jnp.float32)
            line_out[t] = total.astype(jnp.bfloat16)
            out_ref[...] = total

            @pl.when(t < half - 1)
            def _():
                line_copy(t, high, lax.rem(high + 1 + t, half)).start()
                stats_copy(owner, samp).start()

    recv_stats[samp] = send_stats[samp]

    @pl.loop(1, n_samp)
    def _(t):
        stats_copy(samp, lax.rem(samp + n_samp - t, n_samp)).wait_recv()

    first_sums = jnp.zeros((1, owned), jnp.float32)
    square_sums = jnp.zeros((1, owned), jnp.float32)
    for d in range(n_samp):
        first_sums += recv_stats[d, 0:1, :]
        square_sums += recv_stats[d, 1:2, :]
    means = first_sums / total_samples
    variance = square_sums / total_samples - means * means
    turned[n_samp:n_samp + 1, :] = lax.rsqrt(variance + epsilon) / math.sqrt(total_samples)
    for d in range(n_samp):
        turned[d:d + 1, :] = recv_stats[d, 0:1, :] / samples - means

    @pl.loop(0, owned // lanes)
    def _(q):
        span = pl.ds(pl.multiple_of(q * lanes, lanes), lanes)
        columns = turned[:, span].T
        total = out_ref[span, :]
        for d in range(n_samp):
            total += columns[:, d:d + 1] * recv_stats[d, 2:3, 0:lanes]
        out_ref[span, :] = total
        scale[span, :] = jnp.broadcast_to(columns[:, n_samp:n_samp + 1], (lanes, lanes))

    @pl.loop(0, half - 1)
    def _(t):
        source = lax.rem(high + half - 1 - t, half)
        line_copy(t, source, high).wait_recv()
        out_ref[...] += line_in[source].astype(jnp.float32)

    out_ref[...] *= scale[...]

    to_sibling(feat).wait_send()
    for offset in range(1, chips):
        @pl.loop(0, chunks)
        def _(k):
            cross(offset, k, feat, far(offset)).wait_send()
            relay(offset, k, far(chips - offset)).wait_send()

    @pl.loop(0, half)
    def _(t):
        near_copy(t).wait_send()

        @pl.when(t < half - 1)
        def _():
            line_copy(t, high, lax.rem(high + 1 + t, half)).wait_send()

    @pl.loop(1, n_samp)
    def _(t):
        stats_copy(lax.rem(samp + t, n_samp), samp).wait_send()


def per_device(n_feat, n_samp, tier_one, residuals, pair_list):
    rows, samples = tier_one.shape
    pairs = pair_list.shape[1]
    chips = n_feat // 2
    owned = pairs // n_samp
    sub = min(owned // 2, 128)
    chunks = 8
    sizes = (n_feat, n_samp, rows, samples, pairs, chunks)
    dma = pltpu.SemaphoreType.DMA
    return pl.pallas_call(
        functools.partial(kernel, sizes),
        out_shape=jax.ShapeDtypeStruct((owned, lanes), jnp.float32),
        in_specs=[
            pl.BlockSpec(memory_space=pl.ANY),
            pl.BlockSpec(memory_space=pltpu.VMEM),
            pl.BlockSpec(memory_space=pltpu.SMEM),
            pl.BlockSpec(memory_space=pltpu.VMEM),
        ],
        out_specs=pl.BlockSpec(memory_space=pltpu.VMEM),
        scratch_shapes=[
            pltpu.VMEM((n_feat, rows, samples), jnp.bfloat16),
            pltpu.VMEM((n_feat * rows, 4, lanes), jnp.float32),
            pltpu.VMEM((sub * 4, lanes), jnp.float32),
            pltpu.VMEM((sub * 4, lanes), jnp.float32),
            pltpu.VMEM((sub * 4, lanes), jnp.float32),
            pltpu.VMEM((sub * 4, lanes), jnp.float32),
            pltpu.VMEM((pairs, lanes), jnp.int32),
            pltpu.VMEM((samples, 2 * lanes), jnp.bfloat16),
            pltpu.VMEM((owned, lanes), jnp.float32),
            pltpu.VMEM((owned, lanes), jnp.float32),
            pltpu.VMEM((n_samp // 2, owned, lanes), jnp.bfloat16),
            pltpu.VMEM((n_samp // 2, owned, lanes), jnp.bfloat16),
            pltpu.VMEM((n_samp // 2, owned, lanes), jnp.bfloat16),
            pltpu.VMEM((n_samp // 2, owned, lanes), jnp.bfloat16),
            pltpu.VMEM((n_samp, 4, owned), jnp.float32),
            pltpu.VMEM((n_samp, 4, owned), jnp.float32),
            pltpu.VMEM((lanes, owned), jnp.float32),
            pltpu.VMEM((owned, lanes), jnp.float32),
            dma,
            dma((max(chips - 1, 1), chunks)),
            dma((max(chips - 1, 1), chunks)),
            dma,
            dma,
            dma((max(chips - 1, 1), chunks)),
            dma((max(chips - 1, 1), chunks)),
            dma((n_samp // 2,)),
            dma((n_samp // 2,)),
            dma((n_samp // 2,)),
            dma((n_samp // 2,)),
            dma((n_samp,)),
            dma((n_samp,)),
        ],
        compiler_params=pltpu.CompilerParams(
            collective_id=0, has_side_effects=True, vmem_limit_bytes=56 * 2**20
        ),
    )(tier_one, residuals, pair_list, pair_list)


def solution(mesh):
    in_specs = (P("feat", "samp"), P("samp", None), P(None, "feat"))
    out_specs = P(("feat", "samp"), None)
    return jax.shard_map(
        functools.partial(per_device, mesh.shape["feat"], mesh.shape["samp"]),
        mesh=mesh, in_specs=in_specs, out_specs=out_specs, check_vma=False,
    )
```

profile of v0, /device:TPU:0, one launch (start us, length us, event | category | flops | bytes accessed | tf_op | source)
XLA Modules:
  0.0 74.0 jit_solution(733452143332175545)
XLA Ops:
  0.0 72.3 %shard_map.37 = f32[512,128]{1,0:T(8,128)} custom-call(bf16[2048,384]{1,0:T(8,128)(2,1)} %tier_ref.1, bf16[384,128]{1,0:T(8,128)(2,1)} %res_ref.1, s32[3,4096]{1,0:T(4,128)} %pair_vmem.1, s32[3,4096]{1,0:T(4,128)} %pair_vmem.1), custom_call_target="tpu_custom_call" | custom-call | tf_op jit(solution)/shard_map/pallas_call | solution.py:341
  72.3 1.7 %copy.5 = f32[512,128]{1,0:T(8,128)} copy(f32[512,128]{1,0:T(8,128)} %shard_map.37) | data formatting | bytes 524288
where the time goes:
time: 74.2 us; the launch traced here: 74 us
  Pallas kernels  72.3 us (97%)
  local copies, waits for them, and re-layouts  1.67 us (2%)
    pallas_call x1, Pallas kernels, per_device(): pl.pallas_call(functools.partial(kernel, sizes), out_shape=jax.ShapeDtype...  72.3 us
    unnamed x1, local copies, waits for them, and re-layouts  1.67 us

commit v1 on v0

--- a/solution.py
+++ b/solution.py
@@ -149,8 +149,8 @@
         return lax.rem(high + 1 + b, half) * 2 + lax.rem(low + 1 + b // half, 2)
 
     def gather(stages, base, p):
-        firsts = [table[pair_smem[0, base + p + u]] for u in range(group)]
-        seconds = [table[pair_smem[1, base + p + u]] for u in range(group)]
+        firsts = [table[pair_smem[base + (p + u)]] for u in range(group)]
+        seconds = [table[pair_smem[base + (pairs + p + u)]] for u in range(group)]
         for u in range(group):
             stages[0][4 * (p + u):4 * (p + u) + 4, :] = firsts[u]
             stages[1][4 * (p + u):4 * (p + u) + 4, :] = seconds[u]
@@ -195,8 +195,8 @@
     @pl.loop(0, sub // group)
     def _(g):
         base = owner_of(0) * owned
-        firsts = [table[pair_smem[0, base + g * group + u]] for u in range(group)]
-        seconds = [table[pair_smem[1, base + g * group + u]] for u in range(group)]
+        firsts = [table[pair_smem[base + g * group + u]] for u in range(group)]
+        seconds = [table[pair_smem[base + g * group + (pairs + u)]] for u in range(group)]
         for u in range(group):
             spot = pl.ds(pl.multiple_of((g * group + u) * 4, 4), 4)
             first_even[spot, :] = firsts[u]
@@ -384,7 +384,7 @@
         compiler_params=pltpu.CompilerParams(
             collective_id=0, has_side_effects=True, vmem_limit_bytes=56 * 2**20
         ),
-    )(tier_one, residuals, pair_list, pair_list)
+    )(tier_one, residuals, pair_list[:2].reshape(2 * pairs), pair_list)
 
 
 def solution(mesh):

time: 74.2 us -> 70.7 us (0.953); the launches traced: 74 us -> 69.7 us
  Pallas kernels: 72.3 us -> 66.5 us
  local copies, waits for them, and re-layouts: 1.67 us -> 3.14 us
    pallas_call x1, Pallas kernels: 72.3 us -> 66.5 us  [per_device(): pl.pallas_call(functools.partial(kernel, sizes), out_shape=jax.ShapeDtype...]
    unnamed x1 -> x3, local copies, waits for them, and re-layouts: 1.67 us -> 3.14 us
where the time goes in v1:
time: 70.7 us; the launch traced here: 69.7 us
  Pallas kernels  66.5 us (94%)
  local copies, waits for them, and re-layouts  3.14 us (4%)
    pallas_call x1, Pallas kernels, per_device(): pl.pallas_call(functools.partial(kernel, sizes), out_shape=jax.ShapeDtype...  66.5 us
    unnamed x3, local copies, waits for them, and re-layouts  3.14 us

profile of v1, /device:TPU:0, one launch (start us, length us, event | category | flops | bytes accessed | tf_op | source)
XLA Modules:
  0.0 69.7 jit_solution(5152444416022123275)
XLA Ops:
  0.0 0.9 %slice_bitcast_fusion = s32[1,32,2,128]{3,2,1,0:T(2,128)S(1)} fusion(s32[3,4096]{1,0:T(4,128)} %pair_vmem.1), kind=kLoop, calls=%fused_computation | loop fusion | bytes 65536
  0.9 0.6 copy.4
  1.5 66.5 %shard_map.37 = f32[512,128]{1,0:T(8,128)} custom-call(bf16[2048,384]{1,0:T(8,128)(2,1)} %tier_ref.1, bf16[384,128]{1,0:T(8,128)(2,1)} %res_ref.1, s32[8192]{0:T(1024)} %bitcast.3, s32[3,4096]{1,0:T(4,128)} %pair_vmem.1), custom_call_target="tpu_custom_call" | custom-call | tf_op jit(solution)/shard_map/pallas_call | solution.py:341
  68.0 1.7 %copy.6 = f32[512,128]{1,0:T(8,128)} copy(f32[512,128]{1,0:T(8,128)} %shard_map.37) | data formatting | bytes 524288
